TPU v7x, 256 devices: a whole 4x4x8 slice. The times are simulated.
256 devices in a mesh: section: 8 (over y_lo, x), dp: 8 (over z), tensor: 4 (over y_hi, core).
Axes of the slice: x: 4, y: 4 (y_hi: 2, y_lo: 2; y = y_hi * 2 + y_lo), z: 8, core: 2. Of those that a mesh axis runs over, the one named last changes fastest.
Arguments:
- rollout: bfloat16 [16, 256, 5120], P('dp', 'tensor'), may hold values from -6 to 6
- document_ids: int32 [16, 256], P('dp'), may hold values from 0 to 31, never falling along the last dimension, each value on 1 to 128 neighbouring positions
- batch_order: int32 [8, 2], P('dp'), may hold values from 0 to 1, each once within a row
- gains: float32 [8, 5120], P('section'), may hold values from 0.25 to 1.75
- w_query: bfloat16 [8, 5120, 2560], P('section', None, 'tensor'), may hold values from -0.078125 to 0.078125
- bias_query: float32 [8, 2560], P('section', 'tensor'), may hold values from -3 to 3
- w_kv: bfloat16 [8, 2, 5120, 512], P('section', None, None, 'tensor'), may hold values from -0.078125 to 0.078125
- bias_value: float32 [8, 512], P('section', 'tensor'), may hold values from -3 to 3
- w_out: bfloat16 [8, 2560, 5120], P('section', 'tensor', 'dp'), may hold values from -0.125 to 0.125
Outputs:
- hidden_states: bfloat16 [8, 16, 256, 5120], P('section', 'dp', 'tensor')
Inputs may be any that keep to these rules, and one draw needn't show every extreme that they name: `document_ids`: within each micro-batch the document numbers never fall. `batch_order`: each row holds every number of 0 to 1 once.
All inputs are finite; a program needn't handle non-finite values.
Results may differ from a plain program's by a relative error of at most 0.029.
Values may be sent and summed in bfloat16 or wider, within the bound.
A program may use at most 64 MiB of HBM per device.

v0:
```python
import jax
import jax.numpy as jnp
from jax import lax
from jax.sharding import PartitionSpec as P

HD = 128


def passed_along(block, axis, distance):
    devices = range(lax.axis_size(axis))
    route = [(i - distance, i) for i in devices if i - distance in devices]
    return lax.ppermute(block, axis, route)


def normed_rows(rows_piece, gain_row):
    values = rows_piece.astype(jnp.float32)
    meansq = jnp.mean(values * values, axis=-1, keepdims=True)
    return (values * lax.rsqrt(meansq + 1e-06) * gain_row).astype(jnp.bfloat16)


def attend(projected, doc_row, q_width, kv_width):
    tokens = projected.shape[0]
    groups_local = kv_width // HD
    per_group = q_width // kv_width
    query = projected[:, :q_width].reshape(tokens, groups_local, per_group, HD)
    keys = projected[:, q_width : q_width + kv_width].reshape(tokens, groups_local, HD)
    values_mat = projected[:, q_width + kv_width :].reshape(tokens, groups_local, HD)
    scores = jnp.einsum("qgjd,kgd->gjqk", query, keys, preferred_element_type=jnp.float32) * HD ** (
        -0.5
    )
    posit = jnp.arange(tokens)
    allowed = (doc_row[:, None] == doc_row[None, :]) & (posit[:, None] >= posit[None, :])
    scores = jnp.where(allowed[None, None], scores, -1e30)
    top = jnp.max(scores, axis=-1, keepdims=True)
    expo = jnp.exp(scores - top)
    probs = (expo / jnp.sum(expo, axis=-1, keepdims=True)).astype(jnp.bfloat16)
    mixed = jnp.einsum("gjqk,kgd->qgjd", probs, values_mat, preferred_element_type=jnp.float32)
    return mixed.astype(jnp.bfloat16).reshape(tokens, q_width)


def local(rollout, document_ids, batch_order, gains, w_query, bias_query, w_kv, bias_value, w_out):
    micro = rollout.shape[0]
    rows = rollout.shape[1]
    tokens = document_ids.shape[1]
    sections = lax.axis_size("section")
    section_index = lax.axis_index("section")
    total_steps = micro + sections - 1
    gain_row = gains[0]
    wq = w_query[0]
    bq = bias_query[0]
    wk = w_kv[0, 0]
    wv = w_kv[0, 1]
    bv = bias_value[0]
    q_width = wq.shape[1]
    kv_width = wk.shape[1]
    all_width = q_width + 2 * kv_width
    order_row = batch_order[0]
    w_full = lax.all_gather(w_out[0], "dp", axis=1, tiled=True)

    def advance(step_index, carry):
        carried, kept = carry
        slot = step_index - section_index
        active = (slot >= 0) & (slot < micro)
        clipped = jnp.clip(slot, 0, micro - 1)
        local_id = lax.dynamic_index_in_dim(order_row, clipped, 0, keepdims=False)
        doc_row = lax.dynamic_index_in_dim(document_ids, local_id, 0, keepdims=False)
        fresh = lax.dynamic_index_in_dim(rollout, local_id, 0, keepdims=False)
        own_rows = jnp.where(section_index == 0, fresh, carried)

        def project_normal(normal):
            query = jnp.dot(normal, wq, preferred_element_type=jnp.float32) + bq
            keys = jnp.dot(normal, wk, preferred_element_type=jnp.float32)
            values_mat = jnp.dot(normal, wv, preferred_element_type=jnp.float32) + bv
            return jnp.concatenate([query, keys, values_mat], axis=1).astype(jnp.bfloat16)

        def skipped(count):
            return jnp.zeros((count, all_width), jnp.bfloat16)

        rows_piece = lax.all_gather(own_rows, "tensor", axis=0, tiled=True)
        projected = lax.cond(
            active,
            lambda: project_normal(normed_rows(rows_piece, gain_row)),
            lambda: skipped(rows_piece.shape[0]),
        )
        heads_out = lax.cond(
            active,
            lambda: attend(projected, doc_row, q_width, kv_width),
            lambda: jnp.zeros((tokens, q_width), jnp.bfloat16),
        )
        summed = lax.psum_scatter(
            lax.cond(
                active,
                lambda: jnp.dot(heads_out, w_full, preferred_element_type=jnp.float32),
                lambda: jnp.zeros((rows * lax.axis_size("tensor"), w_full.shape[1]), jnp.float32),
            ).astype(jnp.bfloat16),
            "tensor",
            scatter_dimension=0,
            tiled=True,
        ).astype(jnp.float32)
        result = (own_rows.astype(jnp.float32) + summed).astype(jnp.bfloat16)
        previous = lax.dynamic_index_in_dim(kept, clipped, 0, keepdims=False)
        kept = lax.dynamic_update_index_in_dim(
            kept, jnp.where(active, result, previous), clipped, 0
        )
        carried = passed_along(result, "section", 1)
        return (carried, kept)

    stored = jnp.zeros((micro, rows, rollout.shape[2]), jnp.bfloat16)
    start_rows = jnp.zeros((rows, rollout.shape[2]), jnp.bfloat16)
    carried, stored = lax.fori_loop(0, total_steps, advance, (start_rows, stored))
    return stored[None]


def solution(mesh):
    in_specs = (
        P("dp", "tensor", None),
        P("dp", None),
        P("dp", None),
        P("section", None),
        P("section", None, "tensor"),
        P("section", "tensor"),
        P("section", None, None, "tensor"),
        P("section", "tensor"),
        P("section", "tensor", "dp"),
    )
    out_specs = P("section", "dp", "tensor", None)
    return jax.shard_map(local, mesh=mesh, in_specs=in_specs, out_specs=out_specs, check_vma=False)
```

profile of v0, /device:TPU:31, one launch (start us, length us, event | category | flops | bytes accessed | tf_op | source)
XLA Modules:
  0.0 1174.0 jit_solution(6588692909315881377)
XLA Ops:
  10.7 78.1 %all-gather.4.cloned.1.call-done = bf16[1,640,5120]{2,1,0:T(8,128)(2,1)} async-done(((bf16[1,640,640]{2,1,0:T(8,128)(2,1)}), bf16[1,640,5120]{2,1,0:T(8,128)(2,1)}) %all-gather.4.cloned.1.call-update) | async-done | bytes 6553616 | tf_op jit(solution)/shard_map/all_gather | solution.py:58
  90.0 1077.4 %while.16 = (s32[]{:T(128)}, bf16[64,5120]{1,0:T(8,128)(2,1)S(1)}, bf16[2,64,5120]{2,1,0:T(8,128)(2,1)}, pred[]{:T(512)}, s32[]{:T(128)}, /*index=5*/s32[2]{0:T(...) while((s32[]{:T(128)}, bf16[64,5120]{1,0:T(8,128)(2,1)S(1)}, ...), condition=%wide.region_11.12_spmd, body=%wide.region_0.11_spmd.sunk | while | flops 4220712704 | bytes 99988128 | solution.py:110
  94.4 29.7 %all-gather.6.cloned.1.call-done = bf16[256,5120]{1,0:T(8,128)(2,1)} async-done(((bf16[64,5120]{1,0:T(8,128)(2,1)}), bf16[256,5120]{1,0:T(8,128)(2,1)}) %all-gather.6.cloned.1.call-update) | async-done | bytes 2621456 | tf_op jit(solution)/shard_map/while/body/eval_jaxpr/all_gather | solution.py:79
  127.2 58.0 %reduce-scatter.2.cloned.1.call-done = bf16[64,5120]{1,0:T(8,128)(2,1)} async-done(((bf16[256,5120]{1,0:T(8,128)(2,1)}), bf16[64,5120]{1,0:T(8,128)(2,1)}) %reduce-scatter.2.cloned.1.call-update) | async-done | bytes 655376 | tf_op jit(solution)/shard_map/while/body/eval_jaxpr/reduce_scatter | solution.py:90
  188.7 16.2 %collective-permute-done = bf16[64,5120]{1,0:T(8,128)(2,1)S(1)} collective-permute-done((bf16[64,5120]{1,0:T(8,128)(2,1)S(1)}, bf16[64,5120]{1,0:T(8,128)(2,1)S(1)}, u32[]{:S(2)}, u32[]{:S(2)}) %collective-permute-start) | collective-permute-done | bytes 655392 | tf_op jit(solution)/shard_map/while/body/eval_jaxpr/ppermute | solution.py:12
  209.2 33.0 %all-gather.6.cloned.1.call-done = bf16[256,5120]{1,0:T(8,128)(2,1)} async-done(((bf16[64,5120]{1,0:T(8,128)(2,1)}), bf16[256,5120]{1,0:T(8,128)(2,1)}) %all-gather.6.cloned.1.call-update) | async-done | bytes 2621456 | tf_op jit(solution)/shard_map/while/body/eval_jaxpr/all_gather | solution.py:79
  245.3 58.9 %reduce-scatter.2.cloned.1.call-done = bf16[64,5120]{1,0:T(8,128)(2,1)} async-done(((bf16[256,5120]{1,0:T(8,128)(2,1)}), bf16[64,5120]{1,0:T(8,128)(2,1)}) %reduce-scatter.2.cloned.1.call-update) | async-done | bytes 655376 | tf_op jit(solution)/shard_map/while/body/eval_jaxpr/reduce_scatter | solution.py:90
  307.7 16.2 %collective-permute-done = bf16[64,5120]{1,0:T(8,128)(2,1)S(1)} collective-permute-done((bf16[64,5120]{1,0:T(8,128)(2,1)S(1)}, bf16[64,5120]{1,0:T(8,128)(2,1)S(1)}, u32[]{:S(2)}, u32[]{:S(2)}) %collective-permute-start) | collective-permute-done | bytes 655392 | tf_op jit(solution)/shard_map/while/body/eval_jaxpr/ppermute | solution.py:12
  328.2 33.0 %all-gather.6.cloned.1.call-done = bf16[256,5120]{1,0:T(8,128)(2,1)} async-done(((bf16[64,5120]{1,0:T(8,128)(2,1)}), bf16[256,5120]{1,0:T(8,128)(2,1)}) %all-gather.6.cloned.1.call-update) | async-done | bytes 2621456 | tf_op jit(solution)/shard_map/while/body/eval_jaxpr/all_gather | solution.py:79
  364.3 60.4 %reduce-scatter.2.cloned.1.call-done = bf16[64,5120]{1,0:T(8,128)(2,1)} async-done(((bf16[256,5120]{1,0:T(8,128)(2,1)}), bf16[64,5120]{1,0:T(8,128)(2,1)}) %reduce-scatter.2.cloned.1.call-update) | async-done | bytes 655376 | tf_op jit(solution)/shard_map/while/body/eval_jaxpr/reduce_scatter | solution.py:90
  428.1 16.2 %collective-permute-done = bf16[64,5120]{1,0:T(8,128)(2,1)S(1)} collective-permute-done((bf16[64,5120]{1,0:T(8,128)(2,1)S(1)}, bf16[64,5120]{1,0:T(8,128)(2,1)S(1)}, u32[]{:S(2)}, u32[]{:S(2)}) %collective-permute-start) | collective-permute-done | bytes 655392 | tf_op jit(solution)/shard_map/while/body/eval_jaxpr/ppermute | solution.py:12
  448.6 33.0 %all-gather.6.cloned.1.call-done = bf16[256,5120]{1,0:T(8,128)(2,1)} async-done(((bf16[64,5120]{1,0:T(8,128)(2,1)}), bf16[256,5120]{1,0:T(8,128)(2,1)}) %all-gather.6.cloned.1.call-update) | async-done | bytes 2621456 | tf_op jit(solution)/shard_map/while/body/eval_jaxpr/all_gather | solution.py:79
  484.7 60.4 %reduce-scatter.2.cloned.1.call-done = bf16[64,5120]{1,0:T(8,128)(2,1)} async-done(((bf16[256,5120]{1,0:T(8,128)(2,1)}), bf16[64,5120]{1,0:T(8,128)(2,1)}) %reduce-scatter.2.cloned.1.call-update) | async-done | bytes 655376 | tf_op jit(solution)/shard_map/while/body/eval_jaxpr/reduce_scatter | solution.py:90
  548.6 16.2 %collective-permute-done = bf16[64,5120]{1,0:T(8,128)(2,1)S(1)} collective-permute-done((bf16[64,5120]{1,0:T(8,128)(2,1)S(1)}, bf16[64,5120]{1,0:T(8,128)(2,1)S(1)}, u32[]{:S(2)}, u32[]{:S(2)}) %collective-permute-start) | collective-permute-done | bytes 655392 | tf_op jit(solution)/shard_map/while/body/eval_jaxpr/ppermute | solution.py:12
  569.1 33.0 %all-gather.6.cloned.1.call-done = bf16[256,5120]{1,0:T(8,128)(2,1)} async-done(((bf16[64,5120]{1,0:T(8,128)(2,1)}), bf16[256,5120]{1,0:T(8,128)(2,1)}) %all-gather.6.cloned.1.call-update) | async-done | bytes 2621456 | tf_op jit(solution)/shard_map/while/body/eval_jaxpr/all_gather | solution.py:79
  605.2 60.1 %reduce-scatter.2.cloned.1.call-done = bf16[64,5120]{1,0:T(8,128)(2,1)} async-done(((bf16[256,5120]{1,0:T(8,128)(2,1)}), bf16[64,5120]{1,0:T(8,128)(2,1)}) %reduce-scatter.2.cloned.1.call-update) | async-done | bytes 655376 | tf_op jit(solution)/shard_map/while/body/eval_jaxpr/reduce_scatter | solution.py:90
  668.8 16.2 %collective-permute-done = bf16[64,5120]{1,0:T(8,128)(2,1)S(1)} collective-permute-done((bf16[64,5120]{1,0:T(8,128)(2,1)S(1)}, bf16[64,5120]{1,0:T(8,128)(2,1)S(1)}, u32[]{:S(2)}, u32[]{:S(2)}) %collective-permute-start) | collective-permute-done | bytes 655392 | tf_op jit(solution)/shard_map/while/body/eval_jaxpr/ppermute | solution.py:12
  689.3 33.0 %all-gather.6.cloned.1.call-done = bf16[256,5120]{1,0:T(8,128)(2,1)} async-done(((bf16[64,5120]{1,0:T(8,128)(2,1)}), bf16[256,5120]{1,0:T(8,128)(2,1)}) %all-gather.6.cloned.1.call-update) | async-done | bytes 2621456 | tf_op jit(solution)/shard_map/while/body/eval_jaxpr/all_gather | solution.py:79
  725.4 59.5 %reduce-scatter.2.cloned.1.call-done = bf16[64,5120]{1,0:T(8,128)(2,1)} async-done(((bf16[256,5120]{1,0:T(8,128)(2,1)}), bf16[64,5120]{1,0:T(8,128)(2,1)}) %reduce-scatter.2.cloned.1.call-update) | async-done | bytes 655376 | tf_op jit(solution)/shard_map/while/body/eval_jaxpr/reduce_scatter | solution.py:90
  788.4 16.2 %collective-permute-done = bf16[64,5120]{1,0:T(8,128)(2,1)S(1)} collective-permute-done((bf16[64,5120]{1,0:T(8,128)(2,1)S(1)}, bf16[64,5120]{1,0:T(8,128)(2,1)S(1)}, u32[]{:S(2)}, u32[]{:S(2)}) %collective-permute-start) | collective-permute-done | bytes 655392 | tf_op jit(solution)/shard_map/while/body/eval_jaxpr/ppermute | solution.py:12
  808.9 33.0 %all-gather.6.cloned.1.call-done = bf16[256,5120]{1,0:T(8,128)(2,1)} async-done(((bf16[64,5120]{1,0:T(8,128)(2,1)}), bf16[256,5120]{1,0:T(8,128)(2,1)}) %all-gather.6.cloned.1.call-update) | async-done | bytes 2621456 | tf_op jit(solution)/shard_map/while/body/eval_jaxpr/all_gather | solution.py:79
  845.0 61.0 %reduce-scatter.2.cloned.1.call-done = bf16[64,5120]{1,0:T(8,128)(2,1)} async-done(((bf16[256,5120]{1,0:T(8,128)(2,1)}), bf16[64,5120]{1,0:T(8,128)(2,1)}) %reduce-scatter.2.cloned.1.call-update) | async-done | bytes 655376 | tf_op jit(solution)/shard_map/while/body/eval_jaxpr/reduce_scatter | solution.py:90
  909.5 16.2 %collective-permute-done = bf16[64,5120]{1,0:T(8,128)(2,1)S(1)} collective-permute-done((bf16[64,5120]{1,0:T(8,128)(2,1)S(1)}, bf16[64,5120]{1,0:T(8,128)(2,1)S(1)}, u32[]{:S(2)}, u32[]{:S(2)}) %collective-permute-start) | collective-permute-done | bytes 655392 | tf_op jit(solution)/shard_map/while/body/eval_jaxpr/ppermute | solution.py:12
  930.0 33.0 %all-gather.6.cloned.1.call-done = bf16[256,5120]{1,0:T(8,128)(2,1)} async-done(((bf16[64,5120]{1,0:T(8,128)(2,1)}), bf16[256,5120]{1,0:T(8,128)(2,1)}) %all-gather.6.cloned.1.call-update) | async-done | bytes 2621456 | tf_op jit(solution)/shard_map/while/body/eval_jaxpr/all_gather | solution.py:79
  962.9 10.2 conditional.6
  965.5 5.2 fusion.10
  982.2 44.8 %reduce-scatter.2.cloned.1.call-done = bf16[64,5120]{1,0:T(8,128)(2,1)} async-done(((bf16[256,5120]{1,0:T(8,128)(2,1)}), bf16[64,5120]{1,0:T(8,128)(2,1)}) %reduce-scatter.2.cloned.1.call-update) | async-done | bytes 655376 | tf_op jit(solution)/shard_map/while/body/eval_jaxpr/reduce_scatter | solution.py:90
  1030.5 16.2 %collective-permute-done = bf16[64,5120]{1,0:T(8,128)(2,1)S(1)} collective-permute-done((bf16[64,5120]{1,0:T(8,128)(2,1)S(1)}, bf16[64,5120]{1,0:T(8,128)(2,1)S(1)}, u32[]{:S(2)}, u32[]{:S(2)}) %collective-permute-start) | collective-permute-done | bytes 655392 | tf_op jit(solution)/shard_map/while/body/eval_jaxpr/ppermute | solution.py:12
  1051.0 33.0 %all-gather.6.cloned.1.call-done = bf16[256,5120]{1,0:T(8,128)(2,1)} async-done(((bf16[64,5120]{1,0:T(8,128)(2,1)}), bf16[256,5120]{1,0:T(8,128)(2,1)}) %all-gather.6.cloned.1.call-update) | async-done | bytes 2621456 | tf_op jit(solution)/shard_map/while/body/eval_jaxpr/all_gather | solution.py:79
  1084.0 10.2 conditional.6
  1103.3 44.5 %reduce-scatter.2.cloned.1.call-done = bf16[64,5120]{1,0:T(8,128)(2,1)} async-done(((bf16[256,5120]{1,0:T(8,128)(2,1)}), bf16[64,5120]{1,0:T(8,128)(2,1)}) %reduce-scatter.2.cloned.1.call-update) | async-done | bytes 655376 | tf_op jit(solution)/shard_map/while/body/eval_jaxpr/reduce_scatter | solution.py:90
  1151.3 16.2 %collective-permute-done = bf16[64,5120]{1,0:T(8,128)(2,1)S(1)} collective-permute-done((bf16[64,5120]{1,0:T(8,128)(2,1)S(1)}, bf16[64,5120]{1,0:T(8,128)(2,1)S(1)}, u32[]{:S(2)}, u32[]{:S(2)}) %collective-permute-start) | collective-permute-done | bytes 655392 | tf_op jit(solution)/shard_map/while/body/eval_jaxpr/ppermute | solution.py:12
  (219 shorter events, 130.4 us)
Async XLA Ops:
  6.5 82.2 %all-gather.4.cloned.1.call-start = ((), (), s32[]{:S(2)}) async-start(), calls=%async_computation.1 | async-start | bytes 7372800 | tf_op jit(solution)/shard_map/all_gather | solution.py:58
  7.3 82.7 %copy-start.5 = (f32[1,640]{1,0:T(1,128)S(1)}, f32[1,640]{1,0:T(1,128)}, u32[]{:S(2)}) copy-start(f32[1,640]{1,0:T(1,128)} %param.22) | copy-start | bytes 7684
  7.3 82.7 %copy-start.6 = (s32[2,256]{1,0:T(2,128)S(1)}, s32[2,256]{1,0:T(2,128)}, u32[]{:S(2)}) copy-start(s32[2,256]{1,0:T(2,128)} %param.18) | copy-start | bytes 6148
  7.3 82.7 %copy-start.7 = (f32[1,5120]{1,0:T(1,128)S(1)}, f32[1,5120]{1,0:T(1,128)}, u32[]{:S(2)}) copy-start(f32[1,5120]{1,0:T(1,128)} %param.20) | copy-start | bytes 61444
  7.3 82.7 %copy-start.8 = (s32[1,2]{1,0:T(1,128)S(1)}, s32[1,2]{1,0:T(1,128)}, u32[]{:S(2)}) copy-start(s32[1,2]{1,0:T(1,128)} %param.19) | copy-start | bytes 28
  90.1 34.0 %all-gather.6.cloned.1.call-start = ((), (), s32[]{:S(2)}) async-start(), calls=%async_computation.2 | async-start | bytes 3276800 | tf_op jit(solution)/shard_map/while/body/eval_jaxpr/all_gather | solution.py:79
  94.3 90.9 %reduce-scatter.2.cloned.1.call-start = ((), (), s32[]{:S(2)}) async-start(), calls=%async_computation.3 | async-start | bytes 3276800 | tf_op jit(solution)/shard_map/while/body/eval_jaxpr/reduce_scatter | solution.py:90
  187.4 17.5 %collective-permute-start = (bf16[64,5120]{1,0:T(8,128)(2,1)S(1)}, bf16[64,5120]{1,0:T(8,128)(2,1)S(1)}, u32[]{:S(2)}, u32[]{:S(2)}) collective-permute-start(bf16[64,5120]{1,0:T(8,128)(2,1)S(1)} %get-tuple-element.498), channel_id=1, source_target_pairs={{0,32},{32,64},{64,96},{96,128},{128,160},{160,192},{192,224},{1,3... | collective-permute-start | bytes 1966088 | tf_op jit(solution)/shard_map/while/body/eval_jaxpr/ppermute | solution.py:12
  204.9 37.2 %all-gather.6.cloned.1.call-start = ((), (), s32[]{:S(2)}) async-start(), calls=%async_computation.2 | async-start | bytes 3276800 | tf_op jit(solution)/shard_map/while/body/eval_jaxpr/all_gather | solution.py:79
  209.1 95.0 %reduce-scatter.2.cloned.1.call-start = ((), (), s32[]{:S(2)}) async-start(), calls=%async_computation.3 | async-start | bytes 3276800 | tf_op jit(solution)/shard_map/while/body/eval_jaxpr/reduce_scatter | solution.py:90
  306.4 17.5 %collective-permute-start = (bf16[64,5120]{1,0:T(8,128)(2,1)S(1)}, bf16[64,5120]{1,0:T(8,128)(2,1)S(1)}, u32[]{:S(2)}, u32[]{:S(2)}) collective-permute-start(bf16[64,5120]{1,0:T(8,128)(2,1)S(1)} %get-tuple-element.498), channel_id=1, source_target_pairs={{0,32},{32,64},{64,96},{96,128},{128,160},{160,192},{192,224},{1,3... | collective-permute-start | bytes 1966088 | tf_op jit(solution)/shard_map/while/body/eval_jaxpr/ppermute | solution.py:12
  323.9 37.2 %all-gather.6.cloned.1.call-start = ((), (), s32[]{:S(2)}) async-start(), calls=%async_computation.2 | async-start | bytes 3276800 | tf_op jit(solution)/shard_map/while/body/eval_jaxpr/all_gather | solution.py:79
  328.1 96.5 %reduce-scatter.2.cloned.1.call-start = ((), (), s32[]{:S(2)}) async-start(), calls=%async_computation.3 | async-start | bytes 3276800 | tf_op jit(solution)/shard_map/while/body/eval_jaxpr/reduce_scatter | solution.py:90
  426.9 17.5 %collective-permute-start = (bf16[64,5120]{1,0:T(8,128)(2,1)S(1)}, bf16[64,5120]{1,0:T(8,128)(2,1)S(1)}, u32[]{:S(2)}, u32[]{:S(2)}) collective-permute-start(bf16[64,5120]{1,0:T(8,128)(2,1)S(1)} %get-tuple-element.498), channel_id=1, source_target_pairs={{0,32},{32,64},{64,96},{96,128},{128,160},{160,192},{192,224},{1,3... | collective-permute-start | bytes 1966088 | tf_op jit(solution)/shard_map/while/body/eval_jaxpr/ppermute | solution.py:12
  444.3 37.3 %all-gather.6.cloned.1.call-start = ((), (), s32[]{:S(2)}) async-start(), calls=%async_computation.2 | async-start | bytes 3276800 | tf_op jit(solution)/shard_map/while/body/eval_jaxpr/all_gather | solution.py:79
  448.6 96.6 %reduce-scatter.2.cloned.1.call-start = ((), (), s32[]{:S(2)}) async-start(), calls=%async_computation.3 | async-start | bytes 3276800 | tf_op jit(solution)/shard_map/while/body/eval_jaxpr/reduce_scatter | solution.py:90
  547.3 17.5 %collective-permute-start = (bf16[64,5120]{1,0:T(8,128)(2,1)S(1)}, bf16[64,5120]{1,0:T(8,128)(2,1)S(1)}, u32[]{:S(2)}, u32[]{:S(2)}) collective-permute-start(bf16[64,5120]{1,0:T(8,128)(2,1)S(1)} %get-tuple-element.498), channel_id=1, source_target_pairs={{0,32},{32,64},{64,96},{96,128},{128,160},{160,192},{192,224},{1,3... | collective-permute-start | bytes 1966088 | tf_op jit(solution)/shard_map/while/body/eval_jaxpr/ppermute | solution.py:12
  564.8 37.3 %all-gather.6.cloned.1.call-start = ((), (), s32[]{:S(2)}) async-start(), calls=%async_computation.2 | async-start | bytes 3276800 | tf_op jit(solution)/shard_map/while/body/eval_jaxpr/all_gather | solution.py:79
  569.0 96.3 %reduce-scatter.2.cloned.1.call-start = ((), (), s32[]{:S(2)}) async-start(), calls=%async_computation.3 | async-start | bytes 3276800 | tf_op jit(solution)/shard_map/while/body/eval_jaxpr/reduce_scatter | solution.py:90
  667.5 17.5 %collective-permute-start = (bf16[64,5120]{1,0:T(8,128)(2,1)S(1)}, bf16[64,5120]{1,0:T(8,128)(2,1)S(1)}, u32[]{:S(2)}, u32[]{:S(2)}) collective-permute-start(bf16[64,5120]{1,0:T(8,128)(2,1)S(1)} %get-tuple-element.498), channel_id=1, source_target_pairs={{0,32},{32,64},{64,96},{96,128},{128,160},{160,192},{192,224},{1,3... | collective-permute-start | bytes 1966088 | tf_op jit(solution)/shard_map/while/body/eval_jaxpr/ppermute | solution.py:12
  685.0 37.2 %all-gather.6.cloned.1.call-start = ((), (), s32[]{:S(2)}) async-start(), calls=%async_computation.2 | async-start | bytes 3276800 | tf_op jit(solution)/shard_map/while/body/eval_jaxpr/all_gather | solution.py:79
  689.3 95.6 %reduce-scatter.2.cloned.1.call-start = ((), (), s32[]{:S(2)}) async-start(), calls=%async_computation.3 | async-start | bytes 3276800 | tf_op jit(solution)/shard_map/while/body/eval_jaxpr/reduce_scatter | solution.py:90
  787.1 17.5 %collective-permute-start = (bf16[64,5120]{1,0:T(8,128)(2,1)S(1)}, bf16[64,5120]{1,0:T(8,128)(2,1)S(1)}, u32[]{:S(2)}, u32[]{:S(2)}) collective-permute-start(bf16[64,5120]{1,0:T(8,128)(2,1)S(1)} %get-tuple-element.498), channel_id=1, source_target_pairs={{0,32},{32,64},{64,96},{96,128},{128,160},{160,192},{192,224},{1,3... | collective-permute-start | bytes 1966088 | tf_op jit(solution)/shard_map/while/body/eval_jaxpr/ppermute | solution.py:12
  804.6 37.2 %all-gather.6.cloned.1.call-start = ((), (), s32[]{:S(2)}) async-start(), calls=%async_computation.2 | async-start | bytes 3276800 | tf_op jit(solution)/shard_map/while/body/eval_jaxpr/all_gather | solution.py:79
  808.8 97.1 %reduce-scatter.2.cloned.1.call-start = ((), (), s32[]{:S(2)}) async-start(), calls=%async_computation.3 | async-start | bytes 3276800 | tf_op jit(solution)/shard_map/while/body/eval_jaxpr/reduce_scatter | solution.py:90
  908.2 17.5 %collective-permute-start = (bf16[64,5120]{1,0:T(8,128)(2,1)S(1)}, bf16[64,5120]{1,0:T(8,128)(2,1)S(1)}, u32[]{:S(2)}, u32[]{:S(2)}) collective-permute-start(bf16[64,5120]{1,0:T(8,128)(2,1)S(1)} %get-tuple-element.498), channel_id=1, source_target_pairs={{0,32},{32,64},{64,96},{96,128},{128,160},{160,192},{192,224},{1,3... | collective-permute-start | bytes 1966088 | tf_op jit(solution)/shard_map/while/body/eval_jaxpr/ppermute | solution.py:12
  925.7 37.2 %all-gather.6.cloned.1.call-start = ((), (), s32[]{:S(2)}) async-start(), calls=%async_computation.2 | async-start | bytes 3276800 | tf_op jit(solution)/shard_map/while/body/eval_jaxpr/all_gather | solution.py:79
  929.9 97.1 %reduce-scatter.2.cloned.1.call-start = ((), (), s32[]{:S(2)}) async-start(), calls=%async_computation.3 | async-start | bytes 3276800 | tf_op jit(solution)/shard_map/while/body/eval_jaxpr/reduce_scatter | solution.py:90
  1029.2 17.5 %collective-permute-start = (bf16[64,5120]{1,0:T(8,128)(2,1)S(1)}, bf16[64,5120]{1,0:T(8,128)(2,1)S(1)}, u32[]{:S(2)}, u32[]{:S(2)}) collective-permute-start(bf16[64,5120]{1,0:T(8,128)(2,1)S(1)} %get-tuple-element.498), channel_id=1, source_target_pairs={{0,32},{32,64},{64,96},{96,128},{128,160},{160,192},{192,224},{1,3... | collective-permute-start | bytes 1966088 | tf_op jit(solution)/shard_map/while/body/eval_jaxpr/ppermute | solution.py:12
  1046.7 37.3 %all-gather.6.cloned.1.call-start = ((), (), s32[]{:S(2)}) async-start(), calls=%async_computation.2 | async-start | bytes 3276800 | tf_op jit(solution)/shard_map/while/body/eval_jaxpr/all_gather | solution.py:79
  1050.9 96.9 %reduce-scatter.2.cloned.1.call-start = ((), (), s32[]{:S(2)}) async-start(), calls=%async_computation.3 | async-start | bytes 3276800 | tf_op jit(solution)/shard_map/while/body/eval_jaxpr/reduce_scatter | solution.py:90
  1150.0 17.5 %collective-permute-start = (bf16[64,5120]{1,0:T(8,128)(2,1)S(1)}, bf16[64,5120]{1,0:T(8,128)(2,1)S(1)}, u32[]{:S(2)}, u32[]{:S(2)}) collective-permute-start(bf16[64,5120]{1,0:T(8,128)(2,1)S(1)} %get-tuple-element.498), channel_id=1, source_target_pairs={{0,32},{32,64},{64,96},{96,128},{128,160},{160,192},{192,224},{1,3... | collective-permute-start | bytes 1966088 | tf_op jit(solution)/shard_map/while/body/eval_jaxpr/ppermute | solution.py:12
  (25 other events, 646.6 us)
Sparse Core Ops, SparseCore 0:
  9.2 79.5 all-gather.3
  94.5 29.5 all-gather.5
  126.9 58.2 reduce-scatter.1
  209.3 32.8 all-gather.5
  244.8 59.3 reduce-scatter.1
  328.2 32.8 all-gather.5
  363.9 60.6 reduce-scatter.1
  448.7 32.8 all-gather.5
  484.4 60.6 reduce-scatter.1
  569.2 32.8 all-gather.5
  604.9 60.4 reduce-scatter.1
  689.4 32.8 all-gather.5
  725.1 59.7 reduce-scatter.1
  809.0 32.8 all-gather.5
  844.5 61.4 reduce-scatter.1
  930.0 32.8 all-gather.5
  981.2 45.7 reduce-scatter.1
  1051.1 32.8 all-gather.5
  1102.3 45.4 reduce-scatter.1
where the time goes:
time: 1180 us; the launch traced here: 1170 us
  waiting for transfers between devices  1030 us (87%)
  other arithmetic  43.7 us (4%)
  local copies, waits for them, and re-layouts  37.2 us (3%)
  matrix products  26.1 us (2%)
  loops' own time  16.2 us (1%)
  between operations  13.2 us (1%)
  starting transfers between devices  12 us (1%)
    reduce_scatter x9, waiting for transfers between devices, advance(): lax.psum_scatter(lax.cond(active, lambda: jnp.dot(heads_out, w_full, pref...  508 us
    all_gather x9, waiting for transfers between devices, advance(): rows_piece = lax.all_gather(own_rows, 'tensor', axis=0, tiled=True)  293 us
    ppermute x9, waiting for transfers between devices, passed_along(): return lax.ppermute(block, axis, route)  146 us
    all_gather x1, waiting for transfers between devices, local(): w_full = lax.all_gather(w_out[0], 'dp', axis=1, tiled=True)  78.1 us
  transfers between devices with their start and end apart: 28, of which 28 were waited for; matrix products, arithmetic and copies ran while one was open for 1% of the time, Pallas kernels for 0%

commit v1 on v0

v1 whole, which is shorter than its diff:
```python
import functools

import jax
import jax.numpy as jnp
from jax import lax
from jax.experimental import pallas as pl
from jax.experimental.pallas import tpu as pltpu
from jax.sharding import PartitionSpec as P

HD = 128
T = 32
NP = 2
LAGS = 3, 1
MESH = pl.DeviceIdType.MESH


def kernel(
    nsec, ndp, x0, doc_row, doc_col, gains, wq, bq, wkv, bv, w_out, out,
    wcat, wall, xg, hb, xn, pb, pr, kb, vb,
    load_sem, gsend, grecv, fsend, frecv, isend, xrecv, csend, crecv, hsend, hrecv,
    psend, precv, nsend, osend, orecv,
):
    s = lax.axis_index("section")
    z = lax.axis_index("dp")
    t = lax.axis_index("tensor")
    h = t // 2
    c = lax.rem(t, 2)
    micro, rows, width = x0.shape
    tokens = doc_row.shape[2]
    qw = wq.shape[1]
    half = width // 2
    piece = half // NP
    per_mb = tokens // T
    per_own = rows // T
    n = micro * per_mb
    heads = qw // HD
    blk = w_out.shape[1]
    unit = w_out.shape[0] // 2
    sib = {"tensor": 2 * h + 1 - c}
    peer = {"tensor": 2 * (1 - h) + c}
    zright = {"dp": lax.rem(z + 1, ndp)}
    zleft = {"dp": lax.rem(z + ndp - 1, ndp)}

    def remote(src, dst, send, recv, device):
        return pltpu.make_async_remote_copy(
            src_ref=src, dst_ref=dst, send_sem=send, recv_sem=recv,
            device_id=device, device_id_type=MESH,
        )

    loads = []
    for k in range(2):
        base = pl.multiple_of(lax.rem(c + k, 2) * half, half)
        dst = pl.ds(k * half, half)
        loads.append((wq.at[pl.ds(base, half)], wcat.at[dst, pl.ds(0, qw)]))
        for m in range(2):
            loads.append((wkv.at[m, pl.ds(base, half)], wcat.at[dst, pl.ds(qw + m * HD, HD)]))
    loads = [pltpu.make_async_copy(a, b, load_sem.at[k]) for k, (a, b) in enumerate(loads)]

    def place(b, u):
        j = lax.rem(b, 4)
        mine = (b // 4) == c
        slot = jnp.where(mine, j, 4 + j // 2)
        row = jnp.where(mine, 0, lax.rem(j, 2) * (2 * unit)) + u * unit
        return wall.at[slot, pl.ds(pl.multiple_of(row, unit), unit)]

    own_block = [
        pltpu.make_async_copy(w_out.at[pl.ds(u * unit, unit)], place(z, u), load_sem.at[6 + u])
        for u in range(2)
    ]
    for cp in own_block + loads:
        cp.start()

    barrier = pltpu.get_barrier_semaphore()
    partners = [{"tensor": lax.rem(t + k, 4)} for k in range(1, 4)] + [zright, zleft]
    partners += [{"section": lax.rem(s + k, nsec)} for k in (1, nsec - 1)]
    for device in partners:
        pl.semaphore_signal(barrier, inc=1, device_id=device, device_id_type=MESH)
    kb[...] = jnp.zeros_like(kb)
    vb[...] = jnp.zeros_like(vb)
    pl.semaphore_wait(barrier, len(partners))

    def ring(flow, b, k, u):
        return remote(
            place(b, u), place(b, u), gsend.at[flow, k, u], grecv.at[flow, k, u],
            zright if flow == 0 else zleft,
        )

    def to_sib(b, u):
        j = lax.rem(b, 4)
        return remote(
            place(b, u), wall.at[j, pl.ds(pl.multiple_of(2 * unit + u * unit, unit), unit)],
            fsend.at[j, u], frecv.at[j, u], sib,
        )

    for u in range(2):
        own_block[u].wait()
        for flow in range(2):
            ring(flow, z, 0, u).start()

        @pl.when((z // 4) != c)
        def _():
            to_sib(z, u).start()

    def first(j, k, dest, p):
        i = j * per_mb + t * per_own + k
        return (
            x0.at[j, pl.ds(k * T, T), pl.ds(dest % 2 * half + p * piece, piece)],
            xg.at[i, 0, :, pl.ds(p * piece, piece)],
            isend.at[j * per_own + k, dest, p],
            xrecv.at[i, p],
        )

    def firsts(act):
        for j in range(micro):
            for k in range(per_own):
                for p in range(NP):
                    for dest in range(4):
                        src, dst, ssem, rsem = first(j, k, dest, p)

                        @pl.when(dest == t)
                        def _():
                            if act == "start":
                                pltpu.make_async_copy(src, dst, rsem).start()

                        @pl.when(dest != t)
                        def _():
                            cp = remote(src, dst, ssem, rsem, {"tensor": dest})
                            if act == "start":
                                cp.start()
                            else:
                                cp.wait_send()

    @pl.when(s == 0)
    def _():
        firsts("start")

    for cp in loads:
        cp.wait()

    def relay(i, p):
        cols = pl.ds(p * piece, piece)
        return remote(xg.at[i, 0, :, cols], xg.at[i, 1, :, cols], csend.at[i, p], crecv.at[i, p], sib)

    def share(i):
        return remote(hb.at[i, :, pl.ds(0, qw)], hb.at[i, :, pl.ds(qw, qw)], hsend.at[i], hrecv.at[i], sib)

    def exchange(i, k):
        cols = pl.ds(k * piece, piece)
        return remote(pb.at[i, :, cols], pr.at[i, :, cols], psend.at[i, k], precv.at[i, k], peer)

    def hop(i, p):
        cols = pl.ds(p * piece, piece)
        return remote(
            xn.at[i, :, cols], xg.at[i, 0, :, cols], nsend.at[i, p], xrecv.at[i, p],
            {"section": lax.rem(s + 1, nsec)},
        )

    def pass_on(i, p):
        block = xg.at[i, 0, :, pl.ds(p * piece, piece)]
        pltpu.make_async_copy(block, block, xrecv.at[i, p]).wait()
        relay(i, p).start()

    def phase_a(i):
        j = i // per_mb
        r0 = lax.rem(i, per_mb) * T

        def part(k, p):
            x = xg[i, k, :, pl.ds(p * piece, piece)].astype(jnp.float32)
            col = pl.multiple_of(lax.rem(c + k, 2) * half + p * piece, piece)
            g = gains[:, pl.ds(col, piece)]
            sq = jnp.sum(x * x, axis=1, keepdims=True)
            y = jnp.dot(
                (x * g).astype(jnp.bfloat16),
                wcat[pl.ds(k * half + p * piece, piece), :],
                preferred_element_type=jnp.float32,
            )
            return sq, y

        parts = []
        for p in range(NP):
            if p > 0:
                pass_on(i, p)
            parts.append(part(0, p))
        for p in range(NP):
            relay(i, p).wait_recv()
            parts.append(part(1, p))
        sq = sum(a for a, b in parts)
        scale = lax.rsqrt(sq * (1.0 / width) + 1e-6)
        y = sum(b for a, b in parts) * scale
        q = (y[:, :qw] + bq[...]).astype(jnp.bfloat16)
        r0 = pl.multiple_of(r0, T)
        kb[j, pl.ds(r0, T), :] = y[:, qw : qw + HD].astype(jnp.bfloat16)
        vb[j, pl.ds(r0, T), :] = (y[:, qw + HD :] + bv[...]).astype(jnp.bfloat16)
        qs = jnp.concatenate([q[:, k * HD : (k + 1) * HD] for k in range(heads)], axis=0)
        sc = lax.dot_general(
            qs, kb[j], (((1,), (1,)), ((), ())), preferred_element_type=jnp.float32
        ) * HD ** (-0.5)
        dcol = doc_col[j, pl.ds(r0, T), :]
        drow = doc_row[j]
        rowi = lax.broadcasted_iota(jnp.int32, (T, tokens), 0) + r0
        coli = lax.broadcasted_iota(jnp.int32, (T, tokens), 1)
        ok = ((dcol == drow) & (rowi >= coli)).astype(jnp.float32)
        ok = jnp.concatenate([ok] * heads, axis=0) > 0.5
        sc = jnp.where(ok, sc, -1e30)
        top = jnp.max(sc, axis=1, keepdims=True)
        ex = jnp.exp(sc - top)
        probs = (ex / jnp.sum(ex, axis=1, keepdims=True)).astype(jnp.bfloat16)
        o = jnp.dot(probs, vb[j], preferred_element_type=jnp.float32).astype(jnp.bfloat16)
        for k in range(heads):
            hb[i, :, pl.ds(k * HD, HD)] = o[k * T : (k + 1) * T]
        share(i).start()

    def phase_b(i):
        share(i).wait_recv()
        lhs = hb[i]
        for k in range(4):
            y = jnp.dot(lhs, wall[k], preferred_element_type=jnp.float32)
            pb[i, :, pl.ds(k * blk, blk)] = y.astype(jnp.bfloat16)
            if (k + 1) * blk % piece == 0:
                exchange(i, k * blk // piece).start()

    def out_copy(i):
        j = i // per_mb
        r0 = lax.rem(i, per_mb) * T
        owner = r0 // rows
        row = pl.multiple_of(lax.rem(r0, rows), T)
        dst = out.at[j, pl.ds(row, T), pl.ds(pl.multiple_of(c * half, half), half)]
        return owner, xn.at[i], dst, orecv.at[j * per_own + row // T]

    def phase_c(i):
        for p in range(NP):
            cols = pl.ds(p * piece, piece)
            exchange(i, p).wait_recv()
            added = pb[i, :, cols].astype(jnp.float32) + pr[i, :, cols].astype(jnp.float32)
            x = xg[i, 0, :, cols].astype(jnp.float32)
            xn[i, :, cols] = (x + added).astype(jnp.bfloat16)

            @pl.when(s < nsec - 1)
            def _():
                hop(i, p).start()

        owner, src, dst, sem = out_copy(i)

        @pl.when(owner == t)
        def _():
            pltpu.make_async_copy(src, dst, sem).start()

        @pl.when(owner == 2 * h + 1 - c)
        def _():
            remote(src, dst, osend.at[i], sem, sib).start()

    per_step = n // 8

    def gather_step(m, carry):
        k = m // 2
        u = lax.rem(m, 2)
        for flow in range(2):

            @pl.when((k < 3) | (u == flow))
            def _():
                b = lax.rem(z + (ndp - 1 - k if flow == 0 else k + 1), ndp)
                ring(flow, b, k, u).wait_recv()

                @pl.when((k < 2) | ((k == 2) & (u == flow)))
                def _():
                    ring(flow, b, k + 1, u).start()

                @pl.when((b // 4) != c)
                def _():
                    to_sib(b, u).start()

        @pl.when(s == 0)
        def _():
            def both(i, q):
                pass_on(i, 0)
                phase_a(i)
                return q

            lax.fori_loop(m * per_step, (m + 1) * per_step, both, 0)

        return carry

    lax.fori_loop(0, 8, gather_step, 0)
    for j in range(4):
        for u in range(2):
            to_sib(4 * c + j, u).wait_recv()

    lag = jnp.where(s == 0, LAGS[0], LAGS[1])

    @pl.when(s > 0)
    def _():
        pass_on(0, 0)

    def main(i, carry):
        @pl.when((s > 0) & (i < n))
        def _():
            phase_a(i)

        @pl.when(i < n)
        def _():
            phase_b(i)

        @pl.when((s > 0) & (i + 1 < n))
        def _():
            pass_on(i + 1, 0)

        @pl.when(i >= lag)
        def _():
            phase_c(i - lag)

        return carry

    lax.fori_loop(0, n + lag, main, 0)

    for k in range(4):
        for u in range(2):
            for flow in range(2):
                if k < 3 or u == flow:
                    ring(flow, z, k, u).wait_send()
    for j in range(4):
        for u in range(2):
            to_sib(4 * (1 - c) + j, u).wait_send()

    @pl.when(s == 0)
    def _():
        firsts("wait")

    def drain(i, carry):
        share(i).wait_send()
        for k in range(NP):
            relay(i, k).wait_send()
            exchange(i, k).wait_send()

            @pl.when(s < nsec - 1)
            def _():
                hop(i, k).wait_send()

        owner, src, dst, sem = out_copy(i)

        @pl.when(owner == 2 * h + 1 - c)
        def _():
            remote(src, dst, osend.at[i], sem, sib).wait_send()

        return carry

    lax.fori_loop(0, n, drain, 0)
    for j in range(micro):
        for k in range(per_own):
            dst = out.at[j, pl.ds(k * T, T)]
            pltpu.make_async_copy(dst, dst, orecv.at[j * per_own + k]).wait()


def local(nsec, ndp, rollout, document_ids, batch_order, gains, w_query, bias_query, w_kv, bias_value, w_out):
    micro, rows, width = rollout.shape
    tokens = document_ids.shape[1]
    swap = batch_order[0, 0] == 1
    x0 = jnp.where(swap, rollout[::-1], rollout)
    docs = jnp.where(swap, document_ids[::-1], document_ids)
    wq = w_query[0]
    wkv = w_kv[0]
    wo = w_out[0]
    qw = wq.shape[1]
    n = micro * tokens // T
    own = micro * rows // T
    vmem = pl.BlockSpec(memory_space=pltpu.VMEM)
    hbm = pl.BlockSpec(memory_space=pl.ANY)
    bf16 = jnp.bfloat16
    dma = pltpu.SemaphoreType.DMA
    out = pl.pallas_call(
        functools.partial(kernel, nsec, ndp),
        out_shape=jax.ShapeDtypeStruct((micro, rows, width), bf16),
        in_specs=[hbm, vmem, vmem, vmem, hbm, vmem, hbm, vmem, hbm],
        out_specs=hbm,
        scratch_shapes=[
            pltpu.VMEM((width, qw + 2 * HD), bf16),
            pltpu.VMEM((6, 2 * wo.shape[0], wo.shape[1]), bf16),
            pltpu.VMEM((n, 2, T, width // 2), bf16),
            pltpu.VMEM((n, T, 2 * qw), bf16),
            pltpu.VMEM((n, T, width // 2), bf16),
            pltpu.VMEM((n, T, width // 2), bf16),
            pltpu.VMEM((n, T, width // 2), bf16),
            pltpu.VMEM((micro, tokens, HD), bf16),
            pltpu.VMEM((micro, tokens, HD), bf16),
            dma((8,)),
            dma((2, 4, 2)),
            dma((2, 4, 2)),
            dma((4, 2)),
            dma((4, 2)),
            dma((own, 4, NP)),
            dma((n, NP)),
            dma((n, NP)),
            dma((n, NP)),
            dma((n,)),
            dma((n,)),
            dma((n, NP)),
            dma((n, NP)),
            dma((n, NP)),
            dma((n,)),
            dma((own,)),
        ],
        compiler_params=pltpu.CompilerParams(
            collective_id=0, has_side_effects=True, vmem_limit_bytes=48 * 2**20
        ),
        name="layers",
    )(
        x0, docs[:, None, :], docs[:, :, None], gains, wq, bias_query, wkv, bias_value, wo
    )
    return out[None]


def solution(mesh):
    in_specs = (
        P("dp", "tensor", None),
        P("dp", None),
        P("dp", None),
        P("section", None),
        P("section", None, "tensor"),
        P("section", "tensor"),
        P("section", None, None, "tensor"),
        P("section", "tensor"),
        P("section", "tensor", "dp"),
    )
    out_specs = P("section", "dp", "tensor", None)
    body = functools.partial(local, mesh.shape["section"], mesh.shape["dp"])
    return jax.shard_map(body, mesh=mesh, in_specs=in_specs, out_specs=out_specs, check_vma=False)
```

time: 1180 us -> 288 us (0.24)
  waiting for transfers between devices: 1030 us -> 0 us
  Pallas kernels: 0 us -> 283 us
  other arithmetic: 43.7 us -> 2.78 us
  local copies, waits for them, and re-layouts: 37.2 us -> 1.96 us
  matrix products: 26.1 us -> 0 us
  loops' own time: 16.2 us -> 0 us
  between operations: 13.2 us -> 0.74 us
  starting transfers between devices: 12 us -> 0 us
    reduce_scatter x9 -> x0, waiting for transfers between devices: 508 us -> none  [advance(): lax.psum_scatter(lax.cond(active, lambda: jnp.dot(heads_out, w_full, pref...]
    all_gather x10 -> x0, waiting for transfers between devices: 371 us -> none  [the longest x9 293 us: advance(): rows_piece = lax.all_gather(own_rows, 'tensor', axis=0, tiled=True)]
    pallas_call x0 -> x1, Pallas kernels: none -> 283 us  [local(): pl.pallas_call(functools.partial(kernel, nsec, ndp), out_shape=jax.ShapeD...]
    ppermute x9 -> x0, waiting for transfers between devices: 146 us -> none  [passed_along(): return lax.ppermute(block, axis, route)]
    dot_general x12 -> x0, matrix products: 26.1 us -> none  [the longest x2 10.4 us: project_normal(): query = jnp.dot(normal, wq, preferred_element_type=jnp.float32) + bq]
    dynamic_update_slice x9 -> x0, other arithmetic: 19.9 us -> none  [advance(): lax.dynamic_update_index_in_dim(kept, jnp.where(active, result, previous)...]
    another operation x28 -> x0, loops' own time: 16.2 us -> none  [the longest x1 15.6 us: local(): lax.fori_loop(0, total_steps, advance, (start_rows, stored))]
    select_n x9 -> x2, other arithmetic: 18.1 us -> 2.78 us  [the longest x1 2.08 us: local(): x0 = jnp.where(swap, rollout[::-1], rollout)]
  transfers between devices with their start and end apart: 28 -> 0, of which waited for: 28 -> 0; matrix products, arithmetic and copies ran while one was open for 1% -> 0% of each run, Pallas kernels for 0% -> 0%
where the time goes in v1:
time: 288 us
  Pallas kernels  283 us (98%)
    pallas_call x1, Pallas kernels, local(): pl.pallas_call(functools.partial(kernel, nsec, ndp), out_shape=jax.ShapeD...  283 us

profile of v1, /device:TPU:31, one launch (start us, length us, event | category | flops | bytes accessed | tf_op | source)
XLA Modules:
  0.0 288.0 jit_solution(537230675047726595)
XLA Ops:
  0.7 0.7 rev.7
  1.4 0.7 broadcast_select_fusion
  2.1 0.1 copy.11.doc_col
  2.2 0.0 copy-start
  2.2 0.0 copy-start.1
  2.3 0.0 copy-start.2
  2.3 0.0 copy-start.3
  2.3 2.1 reverse_select_fusion.x0
  4.4 0.0 copy-done
  4.4 0.0 copy-done.1
  4.4 0.0 copy-done.2
  4.4 0.0 copy-done.3
  4.4 282.5 %layers.1 = bf16[2,64,5120]{2,1,0:T(8,128)(2,1)S(1)} custom-call(bf16[2,64,5120]{2,1,0:T(8,128)(2,1)S(1)} %reverse_select_fusion.x0, s32[2,1,256]{2,1,0:T(1,128)S(1)} %broadcast_in_dim.9.doc_row, s32[2,256,1]{2,1,0:T(8,128)S(1)} %copy.11.doc_col, f32[1,5120]{1,0:T(1,128)S(1)} %copy-done.1, bf16[5120,640]{1,0:T(8,128)(2,1)} %bitcast.9, ...), custom_call_target="tpu_custom_call" | custom-call | tf_op jit(solution)/shard_map/layers/pallas_call | solution.py:369
  287.0 1.1 copy.13
  (1 shorter events, 0.0 us)
Async XLA Ops:
  2.2 2.1 copy-start
  2.2 2.1 copy-start.1
  2.3 2.1 copy-start.2
  2.3 2.1 copy-start.3

commit v2 on v1

--- a/solution.py
+++ b/solution.py
@@ -15,8 +15,8 @@
 
 
 def kernel(
-    nsec, ndp, x0, doc_row, doc_col, gains, wq, bq, wkv, bv, w_out, out,
-    wcat, wall, xg, hb, xn, pb, pr, kb, vb,
+    nsec, ndp, rollout, order, doc_row, doc_col, gains, wq, bq, wkv, bv, w_out, out,
+    xin, x0, wcat, wall, xg, hb, xn, pb, pr, kb, vb,
     load_sem, gsend, grecv, fsend, frecv, isend, xrecv, csend, crecv, hsend, hrecv,
     psend, precv, nsend, osend, orecv,
 ):
@@ -132,6 +132,11 @@
 
     @pl.when(s == 0)
     def _():
+        cp = pltpu.make_async_copy(rollout, xin, load_sem.at[8])
+        cp.start()
+        cp.wait()
+        for j in range(micro):
+            x0[j] = xin[order[0, j]]
         firsts("start")
 
     for cp in loads:
@@ -354,7 +359,6 @@
     micro, rows, width = rollout.shape
     tokens = document_ids.shape[1]
     swap = batch_order[0, 0] == 1
-    x0 = jnp.where(swap, rollout[::-1], rollout)
     docs = jnp.where(swap, document_ids[::-1], document_ids)
     wq = w_query[0]
     wkv = w_kv[0]
@@ -369,9 +373,11 @@
     out = pl.pallas_call(
         functools.partial(kernel, nsec, ndp),
         out_shape=jax.ShapeDtypeStruct((micro, rows, width), bf16),
-        in_specs=[hbm, vmem, vmem, vmem, hbm, vmem, hbm, vmem, hbm],
+        in_specs=[hbm, pl.BlockSpec(memory_space=pltpu.SMEM), vmem, vmem, vmem, hbm, vmem, hbm, vmem, hbm],
         out_specs=hbm,
         scratch_shapes=[
+            pltpu.VMEM((micro, rows, width), bf16),
+            pltpu.VMEM((micro, rows, width), bf16),
             pltpu.VMEM((width, qw + 2 * HD), bf16),
             pltpu.VMEM((6, 2 * wo.shape[0], wo.shape[1]), bf16),
             pltpu.VMEM((n, 2, T, width // 2), bf16),
@@ -381,7 +387,7 @@
             pltpu.VMEM((n, T, width // 2), bf16),
             pltpu.VMEM((micro, tokens, HD), bf16),
             pltpu.VMEM((micro, tokens, HD), bf16),
-            dma((8,)),
+            dma((9,)),
             dma((2, 4, 2)),
             dma((2, 4, 2)),
             dma((4, 2)),
@@ -403,7 +409,7 @@
         ),
         name="layers",
     )(
-        x0, docs[:, None, :], docs[:, :, None], gains, wq, bias_query, wkv, bias_value, wo
+        rollout, batch_order, docs[:, None, :], docs[:, :, None], gains, wq, bias_query, wkv, bias_value, wo
     )
     return out[None]
 

time: 288 us -> 292 us (1.014)
  local copies, waits for them, and re-layouts: 1.96 us -> 7.12 us
    unnamed x9 -> x13, local copies, waits for them, and re-layouts: 1.08 us -> 6.24 us
where the time goes in v2:
time: 292 us; the launch traced here: 291 us
  Pallas kernels  284 us (97%)
  local copies, waits for them, and re-layouts  7.12 us (2%)
    pallas_call x1, Pallas kernels, local(): pl.pallas_call(functools.partial(kernel, nsec, ndp), out_shape=jax.ShapeD...  284 us
    unnamed x13, local copies, waits for them, and re-layouts  6.24 us

profile of v2, /device:TPU:31, one launch (start us, length us, event | category | flops | bytes accessed | tf_op | source)
XLA Modules:
  0.0 291.4 jit_solution(9205256450079706679)
XLA Ops:
  0.7 0.7 rev.3
  1.4 0.1 copy.11.doc_col
  1.6 0.0 copy-start
  1.6 1.3 copy-done
  2.9 0.0 copy-start.1
  2.9 1.1 copy-done.1
  4.0 0.0 copy-start.2
  4.0 0.7 copy-done.2
  4.8 0.0 copy-start.3
  4.8 0.7 copy-done.3
  5.5 0.0 copy-start.4
  5.5 0.7 copy-done.4
  6.1 0.0 copy-start.5
  6.1 0.7 copy-done.5
  6.8 283.6 %layers.1 = bf16[2,64,5120]{2,1,0:T(8,128)(2,1)S(1)} custom-call(bf16[2,64,5120]{2,1,0:T(8,128)(2,1)S(1)} %copy-done, s32[1,2]{1,0:T(1,128)S(1)} %copy-done.4, s32[2,1,256]{2,1,0:T(1,128)S(1)} %broadcast_in_dim.9.doc_row, s32[2,256,1]{2,1,0:T(8,128)S(1)} %copy.11.doc_col, f32[1,5120]{1,0:T(1,128)S(1)} %copy-done.2, bf16[5120,640]{1,0:T(8,128)(2,1)} %bitcast.10, ...), custom_call_target="tpu_custom_call" | custom-call | tf_op jit(solution)/shard_map/layers/pallas_call | solution.py:373
  290.4 1.1 copy.13
  (2 shorter events, 0.0 us)
Async XLA Ops:
  1.6 1.3 copy-start
  2.9 1.1 copy-start.1
  4.0 0.7 copy-start.2
  4.8 0.7 copy-start.3
  5.5 0.7 copy-start.4
  6.1 0.7 copy-start.5
